TPU v7x, 256 devices: a whole 4x4x8 slice. The times are simulated.
256 devices in a mesh: rows: 32 (over y, z), cols: 8 (over x, core).
Axes of the slice: x: 4, y: 4, z: 8, core: 2. Of those that a mesh axis runs over, the one named last changes fastest.
Arguments:
- x_obs: bfloat16 [12288, 256], P(('rows', 'cols')), may hold values from -2 to 2, as said below
- y_gen: bfloat16 [12288, 256], P(('rows', 'cols')), may hold values from -2 to 2.1, as said below
Outputs:
- divergence: float32 [], replicated
- grad_gen: float32 [12288, 256], P(('rows', 'cols'))
Inputs may be any that keep to these rules, and one draw needn't show every extreme that they name: `x_obs`: coordinates of observed paths. `y_gen`: coordinates of generated paths.
All inputs are finite; a program needn't handle non-finite values.
Results may differ from a plain program's by a relative error of at most 0.0061.
Values may be sent and summed in bfloat16 or wider, within the bound.
A program may use at most 64 MiB of HBM per device.

v0:
```python
import math

import jax
import jax.numpy as jnp
from jax import lax
from jax.sharding import PartitionSpec as P

ITERS = 3


epsilon = 1.0


def pair_costs(left, right):
    cross = lax.dot_general(
        left, right, (((1,), (1,)), ((), ())), preferred_element_type=jnp.float32
    )
    left_f = left.astype(jnp.float32)
    right_f = right.astype(jnp.float32)
    return (
        0.5 * jnp.sum(left_f * left_f, 1)[:, None]
        + 0.5 * jnp.sum(right_f * right_f, 1)[None, :]
        - cross
    )


def across_cols(scores):
    highest = lax.pmax(jnp.stack([jnp.max(score, 1) for score in scores]), "cols")
    summed = jnp.stack(
        [jnp.sum(jnp.exp(score - peak[:, None]), 1) for score, peak in zip(scores, highest)]
    )
    totals = lax.psum(summed, "cols")
    return highest + jnp.log(totals)


def across_rows(scores):
    highest = lax.pmax(jnp.stack([jnp.max(score, 0) for score in scores]), "rows")
    summed = jnp.stack(
        [jnp.sum(jnp.exp(score - peak[None, :]), 0) for score, peak in zip(scores, highest)]
    )
    totals = lax.psum(summed, "rows")
    return highest + jnp.log(totals)


def shards(x_obs, y_gen):
    x_left, y_left = (
        lax.all_gather(x_obs, "cols", axis=0, tiled=True),
        lax.all_gather(y_gen, "cols", axis=0, tiled=True),
    )
    x_right, y_right = (
        lax.all_gather(x_obs, "rows", axis=0, tiled=True),
        lax.all_gather(y_gen, "rows", axis=0, tiled=True),
    )
    shard = x_obs.shape[0]
    points = shard * lax.axis_size("rows") * lax.axis_size("cols")
    log_weight = -math.log(points)
    cost_xy = pair_costs(x_left, y_right)
    cost_xx = pair_costs(x_left, x_right)
    cost_yy = pair_costs(y_left, y_right)
    left_xy = jnp.zeros((x_left.shape[0],), jnp.float32)
    left_xx = left_xy
    left_yy = left_xy
    right_xy = jnp.zeros((x_right.shape[0],), jnp.float32)
    right_xx = right_xy
    right_yy = right_xy
    for step in range(ITERS):
        row_lse = across_cols(
            [
                (right_xy[None, :] - cost_xy) / epsilon,
                (right_xx[None, :] - cost_xx) / epsilon,
                (right_yy[None, :] - cost_yy) / epsilon,
            ]
        )
        left_new = -epsilon * (row_lse + log_weight)
        left_xy = left_new[0]
        col_lse = across_rows(
            [
                (left_xy[:, None] - cost_xy) / epsilon,
                (left_xx[:, None] - cost_xx) / epsilon,
                (left_yy[:, None] - cost_yy) / epsilon,
            ]
        )
        right_new = -epsilon * (col_lse + log_weight)
        right_xy = right_new[0]
        left_xx = 0.5 * (left_xx + left_new[1])
        left_yy = 0.5 * (left_yy + left_new[2])
        right_xx = 0.5 * (right_xx + right_new[1])
        right_yy = 0.5 * (right_yy + right_new[2])
    plan_yy = jnp.exp((left_yy[:, None] + right_yy[None, :] - cost_yy) / epsilon) / points
    plan_yy_low = plan_yy.astype(jnp.bfloat16)
    plan_xy = jnp.exp((left_xy[:, None] + right_xy[None, :] - cost_xy) / epsilon) / points
    plan_xy_low = plan_xy.astype(jnp.bfloat16)
    weight_diff = jnp.sum(plan_xy, 0) - jnp.sum(plan_yy, 0)
    y_part = y_right.astype(jnp.float32)
    moved = lax.dot_general(
        plan_xy_low, x_left, (((0,), (0,)), ((), ())), preferred_element_type=jnp.float32
    )
    moved = moved - lax.dot_general(
        plan_yy_low, y_left, (((0,), (0,)), ((), ())), preferred_element_type=jnp.float32
    )
    grad_gen = lax.psum_scatter(
        y_part * weight_diff[:, None] - moved, "rows", scatter_dimension=0, tiled=True
    )
    left_part = jnp.sum(left_xy - left_xx) / lax.axis_size("cols")
    right_part = jnp.sum(right_xy - right_yy) / lax.axis_size("rows")
    divergence = lax.psum(left_part + right_part, ("rows", "cols")) / points
    return (divergence, grad_gen)


def solution(mesh):
    placed = (P(("rows", "cols"), None), P(("rows", "cols"), None))
    return jax.shard_map(
        shards,
        mesh=mesh,
        in_specs=placed,
        out_specs=(P(), P(("rows", "cols"), None)),
        check_vma=False,
    )
```

profile of v0, /device:TPU:1, one launch (start us, length us, event | category | flops | bytes accessed | tf_op | source)
XLA Modules:
  0.0 1312.4 jit_solution(8963787203019657512)
XLA Ops:
  7.2 16.1 %all_gather.15 = bf16[384,256]{1,0:T(8,128)(2,1)S(1)} all-gather(bf16[48,256]{1,0:T(8,128)(2,1)} %param.3), channel_id=1, replica_groups=mesh['rows'=32,'cols'=8] {'cols'}, dimensions={0}, use_global_device_ids=true | all-gather | bytes 221184 | tf_op jit(solution)/shard_map/all_gather | solution.py:48
  23.3 40.0 %all_gather.13 = bf16[1536,256]{1,0:T(8,128)(2,1)S(1)} all-gather(bf16[48,256]{1,0:T(8,128)(2,1)} %param.3), channel_id=1, replica_groups=mesh['rows'=32,'cols'=8] {'rows'}, dimensions={0}, use_global_device_ids=true | all-gather | bytes 811008 | tf_op jit(solution)/shard_map/all_gather | solution.py:52
  63.3 24.8 %all_gather.12 = bf16[384,256]{1,0:T(8,128)(2,1)S(1)} all-gather(bf16[48,256]{1,0:T(8,128)(2,1)} %param.2), channel_id=1, replica_groups=mesh['rows'=32,'cols'=8] {'cols'}, dimensions={0}, use_global_device_ids=true | all-gather | bytes 221184 | tf_op jit(solution)/shard_map/all_gather | solution.py:47
  88.1 36.5 %all_gather.14 = bf16[1536,256]{1,0:T(8,128)(2,1)S(1)} all-gather(bf16[48,256]{1,0:T(8,128)(2,1)} %param.2), channel_id=1, replica_groups=mesh['rows'=32,'cols'=8] {'rows'}, dimensions={0}, use_global_device_ids=true | all-gather | bytes 811008 | tf_op jit(solution)/shard_map/all_gather | solution.py:51
  125.5 1.9 subtract_reduce_fusion.17
  128.0 1.9 subtract_reduce_fusion.15
  130.0 24.2 %pmax.42 = f32[3,384]{1,0:T(4,128)S(1)} all-reduce(f32[3,384]{1,0:T(4,128)S(1)} %pad_maximum_fusion.6), channel_id=1, replica_groups=mesh['rows'=32,'cols'=8] {'cols'}, use_global_device_ids=true, to_apply=%region_7.0 | all-reduce | flops 1152 | bytes 9216 | tf_op jit(solution)/shard_map/pmax | solution.py:28
  154.2 2.9 subtract_reduce_fusion.14
  158.9 13.2 %psum.49 = f32[3,384]{1,0:T(4,128)} all-reduce(f32[3,384]{1,0:T(4,128)S(1)} %pad_maximum_fusion.7), channel_id=1, replica_groups=mesh['rows'=32,'cols'=8] {'cols'}, use_global_device_ids=true, to_apply=%region_11.0 | all-reduce | flops 1152 | bytes 9216 | tf_op jit(solution)/shard_map/psum | solution.py:32
  172.2 0.7 add_multiply_fusion.5
  172.9 0.6 slice_reduce_fusion.24
  173.8 0.6 pad_maximum_fusion
  174.4 112.5 %pmax.43 = f32[3,1536]{1,0:T(4,128)} all-reduce(f32[3,1536]{1,0:T(4,128)} %pad_maximum_fusion), channel_id=1, replica_groups=mesh['rows'=32,'cols'=8] {'rows'}, use_global_device_ids=true, to_apply=%region_15.0 | all-reduce | flops 4608 | bytes 36864 | tf_op jit(solution)/shard_map/pmax | solution.py:37
  286.9 1.0 slice_reduce_fusion.11
  289.1 0.7 copy-done.9
  290.2 0.6 pad_maximum_fusion.1
  290.8 110.4 %psum.50 = f32[3,1536]{1,0:T(4,128)} all-reduce(f32[3,1536]{1,0:T(4,128)} %pad_maximum_fusion.1), channel_id=1, replica_groups=mesh['rows'=32,'cols'=8] {'rows'}, use_global_device_ids=true, to_apply=%region_19.0 | all-reduce | flops 4608 | bytes 36864 | tf_op jit(solution)/shard_map/psum | solution.py:41
  401.2 0.9 add_multiply_fusion.2
  403.4 1.1 copy-done.10
  404.7 0.6 pad_maximum_fusion.8
  405.3 68.6 %pmax.44 = f32[3,384]{1,0:T(4,128)} all-reduce(f32[3,384]{1,0:T(4,128)} %pad_maximum_fusion.8), channel_id=1, replica_groups=mesh['rows'=32,'cols'=8] {'cols'}, use_global_device_ids=true, to_apply=%region_23.0 | all-reduce | flops 1152 | bytes 9216 | tf_op jit(solution)/shard_map/pmax | solution.py:28
  474.0 0.9 slice_reduce_fusion.23
  474.9 1.4 exponential_reduce_fusion.11
  476.3 1.2 exponential_reduce_fusion.9
  477.5 1.2 exponential_reduce_fusion.10
  478.8 13.2 %psum.51 = f32[3,384]{1,0:T(4,128)} all-reduce(f32[3,384]{1,0:T(4,128)S(1)} %pad_maximum_fusion.9), channel_id=1, replica_groups=mesh['rows'=32,'cols'=8] {'cols'}, use_global_device_ids=true, to_apply=%region_27.0 | all-reduce | flops 1152 | bytes 9216 | tf_op jit(solution)/shard_map/psum | solution.py:32
  492.0 0.7 add_multiply_fusion.4
  492.7 0.7 add_multiply_fusion.7
  493.4 0.7 add_multiply_fusion.8
  494.1 0.7 stack.169
  494.8 0.7 stack.170
  495.8 0.6 pad_maximum_fusion.2
  496.4 110.0 %pmax.45 = f32[3,1536]{1,0:T(4,128)} all-reduce(f32[3,1536]{1,0:T(4,128)} %pad_maximum_fusion.2), channel_id=1, replica_groups=mesh['rows'=32,'cols'=8] {'rows'}, use_global_device_ids=true, to_apply=%region_31.0 | all-reduce | flops 4608 | bytes 36864 | tf_op jit(solution)/shard_map/pmax | solution.py:37
  606.4 1.0 slice_reduce_fusion.7
  608.1 0.6 subtract_reduce_fusion
  609.3 0.6 subtract_reduce_fusion.1
  610.6 0.6 pad_maximum_fusion.3
  611.2 110.3 %psum.52 = f32[3,1536]{1,0:T(4,128)} all-reduce(f32[3,1536]{1,0:T(4,128)} %pad_maximum_fusion.3), channel_id=1, replica_groups=mesh['rows'=32,'cols'=8] {'rows'}, use_global_device_ids=true, to_apply=%region_35.0 | all-reduce | flops 4608 | bytes 36864 | tf_op jit(solution)/shard_map/psum | solution.py:41
  721.5 0.9 add_multiply_fusion.1
  722.4 1.4 slice_reduce_fusion.4
  724.5 1.1 copy-done.4
  725.8 0.6 pad_maximum_fusion.10
  726.4 68.5 %pmax.46 = f32[3,384]{1,0:T(4,128)} all-reduce(f32[3,384]{1,0:T(4,128)} %pad_maximum_fusion.10), channel_id=1, replica_groups=mesh['rows'=32,'cols'=8] {'cols'}, use_global_device_ids=true, to_apply=%region_39.0 | all-reduce | flops 1152 | bytes 9216 | tf_op jit(solution)/shard_map/pmax | solution.py:28
  794.9 0.9 slice_reduce_fusion.19
  795.8 2.2 exponential_reduce_fusion.4
  799.1 0.6 pad_maximum_fusion.11
  799.7 13.3 %psum.53 = f32[3,384]{1,0:T(4,128)} all-reduce(f32[3,384]{1,0:T(4,128)} %pad_maximum_fusion.11), channel_id=1, replica_groups=mesh['rows'=32,'cols'=8] {'cols'}, use_global_device_ids=true, to_apply=%region_43.0 | all-reduce | flops 1152 | bytes 9216 | tf_op jit(solution)/shard_map/psum | solution.py:32
  813.0 0.7 add_multiply_fusion.3
  813.7 0.6 slice_reduce_fusion.12
  814.6 1.3 pad_maximum_fusion.4
  815.9 110.0 %pmax.47 = f32[3,1536]{1,0:T(4,128)} all-reduce(f32[3,1536]{1,0:T(4,128)} %pad_maximum_fusion.4), channel_id=1, replica_groups=mesh['rows'=32,'cols'=8] {'rows'}, use_global_device_ids=true, to_apply=%region_48.0 | all-reduce | flops 4608 | bytes 36864 | tf_op jit(solution)/shard_map/pmax | solution.py:37
  925.9 0.9 slice_reduce_fusion.3
  926.8 2.3 exponential_reduce_fusion.1
  930.1 0.6 pad_maximum_fusion.5
  930.8 110.6 %psum.54 = f32[3,1536]{1,0:T(4,128)} all-reduce(f32[3,1536]{1,0:T(4,128)} %pad_maximum_fusion.5), channel_id=1, replica_groups=mesh['rows'=32,'cols'=8] {'rows'}, use_global_device_ids=true, to_apply=%region_52.0 | all-reduce | flops 4608 | bytes 36864 | tf_op jit(solution)/shard_map/psum | solution.py:41
  1041.3 0.8 add_multiply_fusion
  1042.1 0.7 fusion.19
  1042.9 1.2 fusion.2
  1044.1 1.6 fusion.7
  1046.3 2.2 fusion
  1048.6 0.6 subtract_reduce_fusion.19
  1049.8 0.6 subtract_reduce_fusion.18
  1051.1 127.0 %psum.55 = f32[]{:T(128)} all-reduce(f32[]{:T(128)S(6)} %add.186), channel_id=1, replica_groups=mesh['rows'=32,'cols'=8] {'rows','cols'}, use_global_device_ids=true, to_apply=%region_54.0 | all-reduce | flops 1 | bytes 8 | tf_op jit(solution)/shard_map/psum | solution.py:106
  1178.7 125.7 %reduce-scatter.2.cloned.1.call-done = f32[48,256]{1,0:T(8,128)} async-done(((f32[1536,256]{1,0:T(8,128)}), f32[48,256]{1,0:T(8,128)}) %reduce-scatter.2.cloned.1.call-update) | async-done | bytes 49168 | tf_op jit(solution)/shard_map/reduce_scatter | solution.py:101
  (139 shorter events, 12.5 us)
Async XLA Ops:
  7.2 1297.2 %reduce-scatter.2.cloned.1.call-start = ((), (), s32[]{:S(2)}) async-start(), calls=%async_computation.1 | async-start | bytes 1622016 | tf_op jit(solution)/shard_map/reduce_scatter | solution.py:101
  154.2 3.5 copy-start.8
  172.2 1.6 copy-start.31
  172.2 1.6 copy-start.32
  286.9 1.7 copy-start
  287.9 1.8 copy-start.9
  401.2 1.8 copy-start.1
  402.2 0.6 copy-start.14
  402.8 0.6 copy-start.16
  402.8 1.7 copy-start.10
  474.0 2.3 copy-start.2
  474.0 2.3 copy-start.29
  474.9 2.7 copy-start.11
  474.9 2.7 copy-start.27
  477.5 14.5 %copy-start.19 = (f32[3,384]{1,0:T(4,128)S(1)}, f32[3,384]{1,0:T(4,128)}, u32[]{:S(2)}) copy-start(f32[3,384]{1,0:T(4,128)} %pmax.44) | copy-start | bytes 13828
  493.4 114.4 %copy-start.21 = (f32[384]{0:T(512)}, f32[384]{0:T(512)S(1)}, u32[]{:S(2)}) copy-start(f32[384]{0:T(512)S(1)} %add_multiply_fusion.7) | copy-start | bytes 4612
  494.1 115.2 %copy-start.24 = (f32[384]{0:T(512)}, f32[384]{0:T(512)S(1)}, u32[]{:S(2)}) copy-start(f32[384]{0:T(512)S(1)} %add_multiply_fusion.8) | copy-start | bytes 4612
  495.5 112.3 %copy-start.30 = (f32[384]{0:T(512)S(1)}, f32[384]{0:T(512)}, u32[]{:S(2)}) copy-start(f32[384]{0:T(512)} %get-tuple-element.43) | copy-start | bytes 4612
  606.4 1.7 copy-start.3
  607.3 2.0 copy-start.12
  607.3 2.0 copy-start.28
  721.5 2.6 copy-start.13
  723.9 0.6 copy-start.15
  723.9 1.7 copy-start.4
  794.9 3.1 copy-start.5
  798.5 14.5 %copy-start.20 = (f32[3,384]{1,0:T(4,128)S(1)}, f32[3,384]{1,0:T(4,128)}, u32[]{:S(2)}) copy-start(f32[3,384]{1,0:T(4,128)} %pmax.46) | copy-start | bytes 13828
  799.1 127.7 %copy-start.25 = (f32[384]{0:T(512)S(1)}, f32[384]{0:T(512)}, u32[]{:S(2)}) copy-start(f32[384]{0:T(512)} %copy-done.24) | copy-start | bytes 4612
  814.3 114.8 %copy-start.17 = (f32[384]{0:T(512)}, f32[384]{0:T(512)S(1)}, u32[]{:S(2)}) copy-start(f32[384]{0:T(512)S(1)} %get-tuple-element.32) | copy-start | bytes 4612
  926.8 2.8 copy-start.6
  926.8 2.8 copy-start.22
  1044.1 1.7 copy-start.23
  1044.1 1.7 copy-start.33
  1044.1 1.7 copy-start.7
  1046.3 2.2 copy-start.18
  1046.3 2.2 copy-start.26
  1046.3 2.2 copy-start.34
Sparse Core Ops, SparseCore 0:
  1048.7 255.6 reduce-scatter.1
where the time goes:
time: 1320 us; the launch traced here: 1310 us
  blocking collectives  1110 us (84%)
  waiting for transfers between devices  126 us (10%)
  other arithmetic  38.1 us (3%)
  between operations  17.7 us (1%)
  local copies, waits for them, and re-layouts  13.4 us (1%)
    pmax x3, blocking collectives, across_rows(): lax.pmax(jnp.stack([jnp.max(score, 0) for score in scores]), 'rows')  332 us
    psum x3, blocking collectives, across_rows(): totals = lax.psum(summed, 'rows')  331 us
    pmax x3, blocking collectives, across_cols(): lax.pmax(jnp.stack([jnp.max(score, 1) for score in scores]), 'cols')  161 us
    psum x1, blocking collectives, shards(): divergence = lax.psum(left_part + right_part, ('rows', 'cols')) / points  127 us
    reduce_scatter x1, waiting for transfers between devices, shards(): lax.psum_scatter(y_part * weight_diff[:, None] - moved, 'rows', scatter_d...  126 us
    all_gather x1, blocking collectives, shards(): lax.all_gather(y_gen, 'rows', axis=0, tiled=True)  40 us
    psum x3, blocking collectives, across_cols(): totals = lax.psum(summed, 'cols')  39.8 us
    all_gather x1, blocking collectives, shards(): lax.all_gather(x_obs, 'rows', axis=0, tiled=True)  36.5 us
  transfers between devices with their start and end apart: 1, of which 1 were waited for; matrix products, arithmetic and copies ran while one was open for 0% of the time, Pallas kernels for 0%

commit v1 on v0

v1 whole, which is shorter than its diff:
```python
import functools
import math

import jax
import jax.numpy as jnp
from jax import lax
from jax.experimental import pallas as pl
from jax.experimental.pallas import tpu as pltpu
from jax.sharding import PartitionSpec as P

MESH = pl.DeviceIdType.MESH
LOG2E = math.log2(math.e)
LANES = 128
XY = 4
Z = 8
GROUP = 16

E_XY = (0, 1, 2, 3, 4, 5)
E_YR = (6, 7, 8)
E_YC = (9, 10, 11)
E_XR = (12, 13, 14)
E_XC = (15, 16)
E_SUM = 17
N_EX = 18


def log2(value):
    return jnp.log(value) * LOG2E


def kernel(
    x_ref, y_ref, div_ref, grad_ref,
    xr, xc, yr, yc,
    a_col, a_row, y_col, y_row, x_col, x_row,
    b_f, b_g, b_qr, b_qc, b_pr, b_pc,
    dense, msg, got, low, weights, own_w, o_send, o_got,
    local_sem, bulk_send, bulk_recv, line_recv, ex_send, ex_recv,
):
    shard = x_ref.shape[0]
    block = xr.shape[0]
    tiles = block // LANES
    points = block * GROUP
    log_n = math.log2(points)

    row, col = lax.axis_index("rows"), lax.axis_index("cols")
    px, core = col // 2, col % 2
    py, pz = row // Z, row % Z
    plane_me = px * XY + py
    line_me = pz * 2 + core

    def at(dx, dy, dz, dc):
        x, y, z, c = (px + dx) % XY, (py + dy) % XY, (pz + dz) % Z, (core + dc) % 2
        return (y * Z + z, x * 2 + c)

    plane = [
        (dx, dy, 0, 0)
        for dx, dy in (
            (2, 2), (1, 2), (3, 2), (2, 1), (2, 3), (1, 1), (3, 3), (1, 3), (3, 1),
            (2, 0), (0, 2), (1, 0), (0, 1), (3, 0), (0, 3),
        )
    ]
    hops = (4, 3, 5, 2, 6, 1, 7)
    line = [(0, 0, dz, dc) for dz in hops for dc in (1, 0)] + [(0, 0, 0, 1)]
    plane_at = [at(*p) for p in plane]
    line_at = [at(*p) for p in line]
    line_same = [at(0, 0, dz, 0) for dz in hops]
    sibling = at(0, 0, 0, 1)

    def slot(ref, index):
        return ref.at[pl.ds(pl.multiple_of(index * shard, 16), shard)]

    own = []
    for n, (src, ref, index) in enumerate(
        ((y_ref, yc, plane_me), (x_ref, xr, line_me), (x_ref, xc, plane_me), (y_ref, yr, line_me))
    ):
        copy = pltpu.make_async_copy(src, slot(ref, index), local_sem.at[n])
        copy.start()
        own.append(copy)

    barrier = pltpu.get_barrier_semaphore()
    for peer in plane_at + line_at:
        pl.semaphore_signal(barrier, inc=1, device_id=peer, device_id_type=MESH)
    msg[...] = jnp.zeros_like(msg)
    for copy in own:
        copy.wait()
    pl.semaphore_wait(barrier, len(plane_at) + len(line_at))

    def send_to(src, dst, send, recv, peer):
        copy = pltpu.make_async_remote_copy(
            src_ref=src, dst_ref=dst, send_sem=send, recv_sem=recv, device_id=peer, device_id_type=MESH
        )
        copy.start()
        return copy

    def wait_bytes(ref, sem):
        pltpu.make_async_copy(ref, ref, sem).wait()

    def gather(which, column, rowwise):
        for n in range(len(plane_at)):
            send_to(
                slot(column, plane_me), slot(column, plane_me), bulk_send.at[which], bulk_recv.at[which], plane_at[n]
            )
            if n < len(hops):
                send_to(
                    slot(rowwise, line_me), slot(rowwise, line_me),
                    bulk_send.at[2 + which], line_recv.at[which, n], line_same[n],
                )
        send_to(
            slot(rowwise, line_me), slot(rowwise, line_me), bulk_send.at[2 + which], bulk_recv.at[2 + which], sibling
        )

    def gather_forward(which, rowwise):
        for n in sorted(range(len(hops)), key=lambda n: min(hops[n], Z - hops[n])):
            source = ((pz + Z - hops[n]) % Z) * 2 + core
            part = slot(rowwise, source)
            wait_bytes(part, line_recv.at[which, n])
            send_to(part, part, bulk_send.at[2 + which], bulk_recv.at[2 + which], sibling)

    def gather_wait(which, column, rowwise):
        wait_bytes(column.at[pl.ds(0, 15 * shard)], bulk_recv.at[which])
        wait_bytes(rowwise.at[pl.ds(0, 8 * shard)], bulk_recv.at[2 + which])

    def send(ex, along_line):
        peers, me = (line_at, line_me) if along_line else (plane_at, plane_me)
        for peer in peers:
            send_to(msg.at[ex], got.at[ex, me], ex_send.at[ex], ex_recv.at[ex], peer)
        got[ex, me] = msg[ex]

    def receive(ex):
        wait_bytes(got.at[ex, pl.ds(0, GROUP - 1)], ex_recv.at[ex])

    def combined(ex):
        parts = got[ex]
        peak = jnp.max(parts, 0)
        return peak + log2(jnp.sum(jnp.exp2(parts - peak[None]), 0))

    def spread(index, out):
        def step(k, carry):
            out[pl.ds(pl.multiple_of(k * LANES, LANES), LANES), :] = jnp.broadcast_to(
                dense[index, pl.ds(k, 1), :], (LANES, LANES)
            ).T
            return carry

        lax.fori_loop(0, tiles, step, 0)

    def compact(src, store):
        def step(k, carry):
            store(k, src[pl.ds(pl.multiple_of(k * LANES, LANES), LANES), :].T[0:1, :])
            return carry

        lax.fori_loop(0, tiles, step, 0)

    def half_norms(block_ref, out):
        def step(k, carry):
            rows = pl.ds(pl.multiple_of(k * LANES, LANES), LANES)
            v = block_ref[rows, :].astype(jnp.float32)
            out[rows, :] = jnp.broadcast_to(
                (-0.5 * LOG2E) * jnp.sum(v * v, 1, keepdims=True), (LANES, LANES)
            )
            return carry

        lax.fori_loop(0, tiles, step, 0)

    def products(left, right, out):
        def pair(k, carry):
            both = LOG2E * lax.dot_general(
                left[...],
                right[pl.ds(pl.multiple_of(k * LANES * 2, LANES * 2), LANES * 2), :],
                (((1,), (1,)), ((), ())),
                preferred_element_type=jnp.float32,
            )
            out[2 * k] = both[:, :LANES]
            out[2 * k + 1] = both[:, LANES:]
            return carry

        lax.fori_loop(0, tiles // 2, pair, 0)

    def partial_lse(scores, potential, ex):
        part = 192

        def step(k, carry):
            peak = total = None
            for n in range(block // part):
                rows = pl.ds(n * part, part)
                s = (scores[k, rows, :] + potential[rows, :]).reshape(part // 8, 8, LANES)
                peak_n = jnp.max(s, 0)
                total_n = jnp.sum(jnp.exp2(s - peak_n[None]), 0)
                if peak is None:
                    peak, total = peak_n, total_n
                else:
                    both = jnp.maximum(peak, peak_n)
                    total = total * jnp.exp2(peak - both) + total_n * jnp.exp2(peak_n - both)
                    peak = both
            top = jnp.max(peak, 0, keepdims=True)
            msg[ex, pl.ds(k, 1), :] = top + log2(jnp.sum(total * jnp.exp2(peak - top), 0, keepdims=True))
            return carry

        lax.fori_loop(0, tiles, step, 0)

    D_F, D_G, D_QR, D_QC, D_PR, D_PC = range(6)

    def cross_update(ex, index, out):
        receive(ex)
        dense[index] = log_n - combined(ex)
        if out is not None:
            spread(index, out)

    def self_update(ex, index, out):
        receive(ex)
        dense[index] = 0.5 * (dense[index] + log_n - combined(ex))
        if out is not None:
            spread(index, out)

    def start_dense(index, src):
        def store(k, value):
            dense[index, pl.ds(k, 1), :] = value

        compact(src, store)

    dense[...] = jnp.zeros_like(dense)

    gather(0, yc, xr)
    gather_forward(0, xr)
    gather_wait(0, yc, xr)
    half_norms(yc, b_g)
    products(yc, xr, a_row)
    partial_lse(a_row, b_g, E_XY[0])
    send(E_XY[0], True)
    gather(1, xc, yr)
    products(xr, yc, a_col)
    b_qc[...] = b_g[...]
    start_dense(D_QC, b_qc)
    half_norms(xr, b_pr)
    start_dense(D_PR, b_pr)

    cross_update(E_XY[0], D_F, b_f)
    partial_lse(a_col, b_f, E_XY[1])
    send(E_XY[1], False)

    gather_forward(1, yr)
    gather_wait(1, xc, yr)
    half_norms(yr, b_qr)
    start_dense(D_QR, b_qr)
    products(yc, yr, y_row)
    products(yr, yc, y_col)
    partial_lse(y_row, b_qc, E_YR[0])
    send(E_YR[0], True)
    partial_lse(y_col, b_qr, E_YC[0])
    send(E_YC[0], False)

    cross_update(E_XY[1], D_G, b_g)
    partial_lse(a_row, b_g, E_XY[2])
    send(E_XY[2], True)

    half_norms(xc, b_pc)
    start_dense(D_PC, b_pc)
    products(xc, xr, x_row)
    products(xr, xc, x_col)
    partial_lse(x_row, b_pc, E_XR[0])
    send(E_XR[0], True)
    partial_lse(x_col, b_pr, E_XC[0])
    send(E_XC[0], False)

    cross_update(E_XY[2], D_F, b_f)
    partial_lse(a_col, b_f, E_XY[3])
    send(E_XY[3], False)

    self_update(E_YR[0], D_QR, b_qr)
    self_update(E_YC[0], D_QC, b_qc)
    partial_lse(y_row, b_qc, E_YR[1])
    send(E_YR[1], True)
    partial_lse(y_col, b_qr, E_YC[1])
    send(E_YC[1], False)

    cross_update(E_XY[3], D_G, b_g)
    partial_lse(a_row, b_g, E_XY[4])
    send(E_XY[4], True)

    self_update(E_XR[0], D_PR, b_pr)
    self_update(E_XC[0], D_PC, b_pc)
    partial_lse(x_row, b_pc, E_XR[1])
    send(E_XR[1], True)
    partial_lse(x_col, b_pr, E_XC[1])
    send(E_XC[1], False)
    self_update(E_YR[1], D_QR, b_qr)
    self_update(E_YC[1], D_QC, b_qc)
    partial_lse(y_row, b_qc, E_YR[2])
    send(E_YR[2], True)
    partial_lse(y_col, b_qr, E_YC[2])
    send(E_YC[2], False)

    cross_update(E_XY[4], D_F, None)

    group = 32

    def last_step(n, carry):
        rows = pl.ds(pl.multiple_of(n * group, group), group)
        scores = [a_row[k, rows, :] + dense[D_F, k : k + 1, :] for k in range(tiles)]
        peak = jnp.max(functools.reduce(jnp.maximum, scores), 1, keepdims=True)
        parts = [jnp.exp2(s - peak) for s in scores]
        rounded = [p.astype(jnp.bfloat16) for p in parts]
        total = jnp.sum(functools.reduce(jnp.add, parts), 1, keepdims=True)
        total_low = jnp.sum(functools.reduce(jnp.add, [r.astype(jnp.float32) for r in rounded]), 1, keepdims=True)
        for k in range(tiles):
            low[rows, pl.ds(k * LANES, LANES)] = rounded[k]
        b_f[rows, :] = jnp.broadcast_to(peak + log2(total), (group, LANES))
        b_pc[rows, :] = jnp.broadcast_to(1.0 / total, (group, LANES))
        b_pr[rows, :] = jnp.broadcast_to(total_low, (group, LANES))
        return carry

    lax.fori_loop(0, block // group, last_step, 0)

    def moved(index, scaled, blocks):
        def step(n, carry):
            rows = pl.ds(pl.multiple_of(n * LANES, LANES), LANES)
            product = jnp.dot(low[rows, :], blocks[...], preferred_element_type=jnp.float32)
            for k in range(2):
                lanes = pl.ds(k * LANES, LANES)
                value = product[:, k * LANES : (k + 1) * LANES] - b_pr[rows, :] * yc[rows, lanes].astype(jnp.float32)
                if scaled:
                    value = value * b_pc[rows, :]
                o_send[index, rows, lanes] = value.astype(jnp.bfloat16)
            return carry

        lax.fori_loop(0, block // LANES, step, 0)

    def scatter(index):
        for p, peer in zip(plane, plane_at):
            target = ((px + p[0]) % XY) * XY + (py + p[1]) % XY
            send_to(
                slot(o_send.at[index], target), o_got.at[index, plane_me],
                bulk_send.at[4 + index], bulk_recv.at[4 + index], peer,
            )
        o_got[index, plane_me] = o_send[index, pl.ds(pl.multiple_of(plane_me * shard, 16), shard), :]

    def store_last(k, value):
        msg[E_XY[5], pl.ds(k, 1), :] = value

    compact(b_f, store_last)
    self_update(E_XR[1], D_PR, None)
    self_update(E_XC[1], D_PC, None)
    moved(0, True, xr)
    scatter(0)

    spread(D_PC, b_pc)
    partial_lse(x_row, b_pc, E_XR[2])
    send(E_XR[2], True)
    self_update(E_YR[2], D_QR, b_qr)
    self_update(E_YC[2], D_QC, b_qc)

    def plan_step(n, carry):
        rows = pl.ds(pl.multiple_of(n * group, group), group)
        total = None
        for k in range(tiles):
            plan = jnp.exp2(y_row[k, rows, :] + (dense[D_QR, k : k + 1, :] - log_n) + b_qc[rows, :])
            low[rows, pl.ds(k * LANES, LANES)] = plan.astype(jnp.bfloat16)
            total = plan if total is None else total + plan
        b_pr[rows, :] = jnp.broadcast_to(jnp.sum(total, 1, keepdims=True), (group, LANES))
        return carry

    lax.fori_loop(0, block // group, plan_step, 0)
    moved(1, False, yr)
    scatter(1)
    self_update(E_XR[2], D_PR, None)

    used = lax.broadcasted_iota(jnp.int32, (8, LANES), 0) < tiles
    here = jnp.where(used, dense[D_F] - dense[D_PR] - dense[D_QR], 0.0)
    msg[E_XY[5], pl.ds(tiles, 1), :] = jnp.sum(here, 0, keepdims=True)
    send(E_XY[5], False)

    receive(E_XY[5])
    parts = got[E_XY[5]]
    lse = combined(E_XY[5])
    dense[D_G] = log_n - lse
    weights[...] = jnp.exp2(parts - lse[None])
    msg[E_SUM] = jnp.where(used, dense[D_G], 0.0)
    send(E_SUM, True)
    others = jnp.sum(parts, 0)[tiles : tiles + 1, :]
    for k in range(tiles):
        rows = jnp.concatenate([weights[:, k, :], jnp.zeros((LANES - GROUP, LANES), jnp.float32)], 0)
        own_w[pl.ds(k * LANES, LANES), :] = rows.T
    mine = own_w[pl.ds(pl.multiple_of(plane_me * shard, 16), shard), :]

    wait_bytes(o_got.at[0, pl.ds(0, GROUP - 1)], bulk_recv.at[4])
    wait_bytes(o_got.at[1, pl.ds(0, GROUP - 1)], bulk_recv.at[5])
    grad = jnp.zeros(grad_ref.shape, jnp.float32)
    for n in range(GROUP):
        grad = grad + o_got[1, n].astype(jnp.float32)
        grad = grad - mine[:, n : n + 1] * o_got[0, n].astype(jnp.float32)
    grad_ref[...] = grad

    receive(E_SUM)
    total = jnp.sum(jnp.sum(got[E_SUM], 0), 0, keepdims=True) + others
    div_ref[...] = jnp.broadcast_to(
        jnp.sum(total, 1, keepdims=True) * (1.0 / (LOG2E * points)), div_ref.shape
    )

    for which, (column, rowwise) in enumerate(((yc, xr), (xc, yr))):
        wait_bytes(column.at[pl.ds(0, 15 * shard)], bulk_send.at[which])
        wait_bytes(rowwise.at[pl.ds(0, 15 * shard)], bulk_send.at[2 + which])
    for index in range(2):
        wait_bytes(o_got.at[index, pl.ds(0, GROUP - 1)], bulk_send.at[4 + index])
    for ex in range(N_EX):
        wait_bytes(got.at[ex, pl.ds(0, GROUP - 1)], ex_send.at[ex])


def shards(x_obs, y_gen):
    shard, width = x_obs.shape
    block = shard * GROUP
    tiles = block // LANES
    f32, bf16 = jnp.float32, jnp.bfloat16
    div, grad = pl.pallas_call(
        kernel,
        out_shape=(jax.ShapeDtypeStruct((8, LANES), f32), jax.ShapeDtypeStruct((shard, width), f32)),
        in_specs=[pl.BlockSpec(memory_space=pl.ANY)] * 2,
        out_specs=(pl.BlockSpec(memory_space=pltpu.VMEM), pl.BlockSpec(memory_space=pltpu.VMEM)),
        scratch_shapes=[
            *[pltpu.VMEM((block, width), bf16)] * 4,
            *[pltpu.VMEM((tiles, block, LANES), f32)] * 6,
            *[pltpu.VMEM((block, LANES), f32)] * 6,
            pltpu.VMEM((6, 8, LANES), f32),
            pltpu.VMEM((N_EX, 8, LANES), f32),
            pltpu.VMEM((N_EX, GROUP, 8, LANES), f32),
            pltpu.VMEM((block, block), bf16),
            pltpu.VMEM((GROUP, 8, LANES), f32),
            pltpu.VMEM((block, LANES), f32),
            pltpu.VMEM((2, block, width), bf16),
            pltpu.VMEM((2, GROUP, shard, width), bf16),
            pltpu.SemaphoreType.DMA((4,)),
            pltpu.SemaphoreType.DMA((6,)),
            pltpu.SemaphoreType.DMA((6,)),
            pltpu.SemaphoreType.DMA((2, 7)),
            pltpu.SemaphoreType.DMA((N_EX,)),
            pltpu.SemaphoreType.DMA((N_EX,)),
        ],
        compiler_params=pltpu.CompilerParams(
            collective_id=0, has_side_effects=True, vmem_limit_bytes=48 * 1024 * 1024
        ),
    )(x_obs, y_gen)
    return div[0, 0], grad


def solution(mesh):
    placed = P(("rows", "cols"), None)
    return jax.shard_map(
        shards, mesh=mesh, in_specs=(placed, placed), out_specs=(P(), placed), check_vma=False
    )
```

time: 1320 us -> 81.5 us (0.06)
  blocking collectives: 1110 us -> 0 us
  waiting for transfers between devices: 126 us -> 0 us
  Pallas kernels: 0 us -> 78.1 us
  other arithmetic: 38.1 us -> 0 us
  between operations: 17.7 us -> 0.65 us
    psum x7 -> x0, blocking collectives: 498 us -> none  [the longest x3 331 us: across_rows(): totals = lax.psum(summed, 'rows')]
    pmax x6 -> x0, blocking collectives: 494 us -> none  [the longest x3 332 us: across_rows(): lax.pmax(jnp.stack([jnp.max(score, 0) for score in scores]), 'rows')]
    reduce_scatter x1 -> x0, waiting for transfers between devices: 126 us -> none  [shards(): lax.psum_scatter(y_part * weight_diff[:, None] - moved, 'rows', scatter_d...]
    all_gather x4 -> x0, blocking collectives: 117 us -> none  [the longest x1 40 us: shards(): lax.all_gather(y_gen, 'rows', axis=0, tiled=True)]
    pallas_call x0 -> x1, Pallas kernels: none -> 78.1 us  [shards(): pl.pallas_call(kernel, out_shape=(jax.ShapeDtypeStruct((8, LANES), f32),...]
    reduce_sum x21 -> x0, other arithmetic: 15.9 us -> none  [the longest x6 7.08 us: across_cols(): jnp.sum(jnp.exp(score - peak[:, None]), 1)]
  transfers between devices with their start and end apart: 1 -> 0, of which waited for: 1 -> 0; matrix products, arithmetic and copies ran while one was open for 0% -> 0% of each run, Pallas kernels for 0% -> 0%
where the time goes in v1:
time: 81.5 us; the launch traced here: 81.3 us
  Pallas kernels  78.1 us (96%)
  local copies, waits for them, and re-layouts  2.6 us (3%)
    pallas_call x1, Pallas kernels, shards(): pl.pallas_call(kernel, out_shape=(jax.ShapeDtypeStruct((8, LANES), f32),...  78.1 us
    unnamed x5, local copies, waits for them, and re-layouts  2.09 us

profile of v1, /device:TPU:1, one launch (start us, length us, event | category | flops | bytes accessed | tf_op | source)
XLA Modules:
  0.0 81.3 jit_solution(8517798882056046293)
XLA Ops:
  0.6 0.0 copy-start
  0.6 0.7 copy-done
  1.4 0.0 copy-start.1
  1.4 0.7 copy-done.1
  2.1 78.1 %shard_map.41 = (f32[8,128]{1,0:T(8,128)S(1)}, f32[48,256]{1,0:T(8,128)S(1)}) custom-call(bf16[48,256]{1,0:T(8,128)(2,1)S(1)} %copy-done, bf16[48,256]{1,0:T(8,128)(2,1)S(1)} %copy-done.1), custom_call_target="tpu_custom_call" | custom-call | tf_op jit(solution)/shard_map/pallas_call | solution.py:412
  80.2 0.5 slice.3
  80.7 0.6 copy.5
Async XLA Ops:
  0.6 0.7 copy-start
  1.4 0.7 copy-start.1

commit v2 on v1

v2 whole, which is shorter than its diff:
```python
import math

import jax
import jax.numpy as jnp
from jax import lax
from jax.experimental import pallas as pl
from jax.experimental.pallas import tpu as pltpu
from jax.sharding import PartitionSpec as P

MESH = pl.DeviceIdType.MESH
LOG2E = math.log2(math.e)
LANES = 128
XY = 4
Z = 8
GROUP = 16

E_XY = (0, 1, 2, 3, 4, 5)
E_YR = (6, 7, 8)
E_YC = (9, 10, 11)
E_XR = (12, 13)
E_XC = (14, 15, 16)
E_SUM = 17
N_EX = 18


def log2(value):
    return jnp.log(value) * LOG2E


def kernel(
    x_ref, y_ref, div_ref, grad_ref,
    xr, xc, yr, yc,
    a_col, a_row, y_own, x_own,
    b_f, b_g, b_ny, b_nx, b_vy, b_vx,
    dense, msg, got, weights, own_w, o_send, o_got,
    local_sem, bulk_send, bulk_recv, line_recv, ex_send, ex_recv,
):
    shard = xr.shape[0] // GROUP
    block = xr.shape[0]
    tiles = block // LANES
    points = block * GROUP
    log_n = math.log2(points)

    row, col = lax.axis_index("rows"), lax.axis_index("cols")
    px, core = col // 2, col % 2
    py, pz = row // Z, row % Z
    plane_me = px * XY + py
    line_me = pz * 2 + core

    def at(dx, dy, dz, dc):
        x, y, z, c = (px + dx) % XY, (py + dy) % XY, (pz + dz) % Z, (core + dc) % 2
        return (y * Z + z, x * 2 + c)

    plane = [
        (dx, dy, 0, 0)
        for dx, dy in (
            (2, 2), (1, 2), (3, 2), (2, 1), (2, 3), (1, 1), (3, 3), (1, 3), (3, 1),
            (2, 0), (0, 2), (1, 0), (0, 1), (3, 0), (0, 3),
        )
    ]
    hops = (4, 3, 5, 2, 6, 1, 7)
    line = [(0, 0, dz, dc) for dz in hops for dc in (1, 0)] + [(0, 0, 0, 1)]
    plane_at = [at(*p) for p in plane]
    line_at = [at(*p) for p in line]
    line_same = [at(0, 0, dz, 0) for dz in hops]
    sibling = at(0, 0, 0, 1)

    def slot(ref, index):
        return ref.at[pl.ds(pl.multiple_of(index * shard, 16), shard)]

    barrier = pltpu.get_barrier_semaphore()
    for peer in line_at + plane_at:
        pl.semaphore_signal(barrier, inc=1, device_id=peer, device_id_type=MESH)

    own = []
    for n, (src, ref, index) in enumerate(
        ((y_ref, yc, plane_me), (x_ref, xr, line_me), (x_ref, xc, plane_me), (y_ref, yr, line_me))
    ):
        copy = pltpu.make_async_copy(src, slot(ref, index), local_sem.at[n])
        copy.start()
        own.append(copy)
    msg[...] = jnp.ones_like(msg)
    dense[...] = jnp.ones_like(dense)
    b_vy[...] = jnp.ones_like(b_vy)
    b_vx[...] = jnp.ones_like(b_vx)
    for copy in own:
        copy.wait()
    pl.semaphore_wait(barrier, len(plane_at) + len(line_at))

    def send_to(src, dst, send, recv, peer):
        copy = pltpu.make_async_remote_copy(
            src_ref=src, dst_ref=dst, send_sem=send, recv_sem=recv, device_id=peer, device_id_type=MESH
        )
        copy.start()
        return copy

    def wait_bytes(ref, sem):
        pltpu.make_async_copy(ref, ref, sem).wait()

    def send_plane(which, column, n):
        send_to(slot(column, plane_me), slot(column, plane_me), bulk_send.at[which], bulk_recv.at[which], plane_at[n])

    def send_line(which, rowwise, n):
        part = slot(rowwise, line_me)
        if n < len(hops):
            send_to(part, part, bulk_send.at[2 + which], line_recv.at[which, n], line_same[n])
        else:
            send_to(part, part, bulk_send.at[2 + which], bulk_recv.at[2 + which], sibling)

    def gather(which, column, rowwise):
        for n in range(len(plane_at)):
            if rowwise is not None and n <= len(hops):
                send_line(which, rowwise, n)
            if column is not None:
                send_plane(which, column, n)

    def gather_forward(which, rowwise):
        for n in sorted(range(len(hops)), key=lambda n: min(hops[n], Z - hops[n])):
            source = ((pz + Z - hops[n]) % Z) * 2 + core
            part = slot(rowwise, source)
            wait_bytes(part, line_recv.at[which, n])
            send_to(part, part, bulk_send.at[2 + which], bulk_recv.at[2 + which], sibling)

    def gather_plane(which, column):
        wait_bytes(column.at[pl.ds(0, 15 * shard)], bulk_recv.at[which])

    def gather_line(which, rowwise):
        wait_bytes(rowwise.at[pl.ds(0, 8 * shard)], bulk_recv.at[2 + which])

    def send(ex, along_line):
        peers, me = (line_at, line_me) if along_line else (plane_at, plane_me)
        for peer in peers:
            send_to(msg.at[ex], got.at[ex, me], ex_send.at[ex], ex_recv.at[ex], peer)
        got[ex, me] = msg[ex]

    def receive(ex):
        wait_bytes(got.at[ex, pl.ds(0, GROUP - 1)], ex_recv.at[ex])

    def combined(ex):
        parts = got[ex]
        peak = jnp.max(parts, 0)
        return peak + log2(jnp.sum(jnp.exp2(parts - peak[None]), 0))

    def spread(index, out):
        for k in range(tiles):
            out[k * LANES : (k + 1) * LANES, :] = jnp.broadcast_to(dense[index, k : k + 1, :], (LANES, LANES)).T

    def half_norms(block_ref, out, index):
        v = block_ref[...].astype(jnp.float32)
        v = v * v
        high = v.astype(jnp.bfloat16)
        rest = (v - high.astype(jnp.float32)).astype(jnp.bfloat16)
        if out is not None:
            ones = jnp.full((v.shape[1], LANES), 1.0, jnp.bfloat16)
            out[...] = (-0.5 * LOG2E) * (
                jnp.dot(high, ones, preferred_element_type=jnp.float32)
                + jnp.dot(rest, ones, preferred_element_type=jnp.float32)
            )
        if index is not None:
            ones = jnp.full((8, v.shape[1]), 1.0, jnp.bfloat16)
            dims = (((1,), (1,)), ((), ()))
            value = (-0.5 * LOG2E) * (
                lax.dot_general(ones, high, dims, preferred_element_type=jnp.float32)
                + lax.dot_general(ones, rest, dims, preferred_element_type=jnp.float32)
            )
            for k in range(tiles):
                dense[index, k : k + 1, :] = value[0:1, k * LANES : (k + 1) * LANES]

    def products(left, right, out, norm_left=None, norm_right=None):
        wide = 2 * LANES
        for k in range(0, tiles, 2):
            both = LOG2E * lax.dot_general(
                left[...],
                right[k * LANES : k * LANES + wide, :],
                (((1,), (1,)), ((), ())),
                preferred_element_type=jnp.float32,
            )
            for h in range(2):
                part = both[:, h * LANES : (h + 1) * LANES]
                if norm_left is not None:
                    part = jnp.exp2(part + norm_left[...] + dense[norm_right, k + h : k + h + 1, :])
                out[k + h] = part

    def partial_lse(scores, potential, ex):
        part, together = 64, 3

        def step(first, carry):
            state = [None] * together
            for n in range(block // part):
                rows = pl.ds(n * part, part)
                p = potential[rows, :]
                for u in range(together):
                    s = (scores[first * together + u, rows, :] + p).reshape(part // 8, 8, LANES)
                    peak = jnp.max(s, 0)
                    total = jnp.sum(jnp.exp2(s - peak[None]), 0)
                    if n:
                        both = jnp.maximum(state[u][0], peak)
                        total = state[u][1] * jnp.exp2(state[u][0] - both) + total * jnp.exp2(peak - both)
                        peak = both
                    state[u] = (peak, total)
            for u, (peak, total) in enumerate(state):
                top = jnp.max(peak, 0, keepdims=True)
                msg[ex, pl.ds(first * together + u, 1), :] = top + log2(
                    jnp.sum(total * jnp.exp2(peak - top), 0, keepdims=True)
                )
            return carry

        lax.fori_loop(0, tiles // together, step, 0)

    def self_sums(kernel_ref, v_column, v_row, ex_row, ex_col):
        part, together = 32, 3

        def step(first, carry):
            down = list(carry)
            for u in range(together):
                n = first * together + u
                across = []
                for g in range(LANES // part):
                    rows = pl.ds(pl.multiple_of(n * LANES + g * part, part), part)
                    total = None
                    for k in range(tiles):
                        tile = kernel_ref[k, rows, :]
                        if ex_row is not None:
                            down[k] = down[k] + jnp.sum((tile * v_column[rows, :]).reshape(part // 8, 8, LANES), 0)
                        term = tile * dense[v_row, k : k + 1, :]
                        total = term if total is None else total + term
                    across.append(total)
                msg[ex_col, pl.ds(n, 1), :] = jnp.sum(jnp.concatenate(across, 0).T, 0, keepdims=True)
            return tuple(down)

        first = tuple(jnp.zeros((8, LANES), jnp.float32) for _ in range(tiles if ex_row is not None else 0))
        down = lax.fori_loop(0, tiles // together, step, first)
        for k, value in enumerate(down):
            msg[ex_row, k : k + 1, :] = jnp.sum(value, 0, keepdims=True)

    D_F, D_G, D_NX, D_NY, D_VXR, D_VXC, D_VYR, D_VYC = range(8)

    def cross_update(ex, index, out):
        receive(ex)
        dense[index] = log_n - combined(ex)
        if out is not None:
            spread(index, out)

    def self_update(ex, index, out):
        receive(ex)
        dense[index] = jnp.sqrt(dense[index] * points / jnp.sum(got[ex], 0))
        if out is not None:
            spread(index, out)

    def moved(index, weight, rows_ref):
        quarter = shard * XY
        ones = jnp.full((block, LANES), 1.0, jnp.bfloat16)
        for dx in (2, 1, 3, 0):
            qx = (px + dx) % XY
            rows = pl.ds(pl.multiple_of(qx * quarter, 16), quarter)
            low = jnp.concatenate([weight(k, rows).astype(jnp.bfloat16) for k in range(tiles)], 1)
            product = jnp.dot(low, rows_ref[...], preferred_element_type=jnp.float32)
            total = jnp.dot(low, ones, preferred_element_type=jnp.float32)
            for k in range(2):
                lanes = pl.ds(k * LANES, LANES)
                value = product[:, k * LANES : (k + 1) * LANES] - total * yc[rows, lanes].astype(jnp.float32)
                o_send[index, rows, lanes] = value.astype(jnp.bfloat16)
            for dy in (2, 1, 3, 0):
                if dx or dy:
                    send_to(
                        slot(o_send.at[index], qx * XY + (py + dy) % XY), o_got.at[index, plane_me],
                        bulk_send.at[4 + index], bulk_recv.at[4 + index], at(dx, dy, 0, 0),
                    )
        o_got[index, plane_me] = o_send[index, pl.ds(pl.multiple_of(plane_me * shard, 16), shard), :]

    def plan_yy(k, rows):
        return y_own[k, rows, :] * (dense[D_VYR, k : k + 1, :] * (1.0 / points)) * b_vy[rows, :]

    def plan_xy(k, rows):
        return jnp.exp2(a_row[k, rows, :] + dense[D_F, k : k + 1, :] - b_g[rows, :])

    gather(0, yc, xr)
    gather(1, None, yr)
    gather_forward(0, xr)
    gather_plane(0, yc)
    half_norms(yc, b_ny, None)
    gather_line(0, xr)
    products(yc, xr, a_row)
    partial_lse(a_row, b_ny, E_XY[0])
    send(E_XY[0], True)

    gather(1, xc, None)
    products(xr, yc, a_col)
    half_norms(xr, None, D_NX)
    gather_forward(1, yr)
    gather_line(1, yr)
    half_norms(yr, None, D_NY)
    products(yc, yr, y_own, b_ny, D_NY)
    self_sums(y_own, b_vy, D_VYR, E_YR[0], E_YC[0])
    send(E_YR[0], True)
    send(E_YC[0], False)

    cross_update(E_XY[0], D_F, b_f)
    partial_lse(a_col, b_f, E_XY[1])
    send(E_XY[1], False)

    gather_plane(1, xc)
    half_norms(xc, b_nx, None)
    products(xc, xr, x_own, b_nx, D_NX)
    self_sums(x_own, b_vx, D_VXR, E_XR[0], E_XC[0])
    send(E_XR[0], True)
    send(E_XC[0], False)

    cross_update(E_XY[1], D_G, b_g)
    partial_lse(a_row, b_g, E_XY[2])
    send(E_XY[2], True)

    self_update(E_YR[0], D_VYR, None)
    self_update(E_YC[0], D_VYC, b_vy)
    self_sums(y_own, b_vy, D_VYR, E_YR[1], E_YC[1])
    send(E_YR[1], True)
    send(E_YC[1], False)

    cross_update(E_XY[2], D_F, b_f)
    partial_lse(a_col, b_f, E_XY[3])
    send(E_XY[3], False)

    self_update(E_YR[1], D_VYR, None)
    self_update(E_YC[1], D_VYC, b_vy)
    self_sums(y_own, b_vy, D_VYR, E_YR[2], E_YC[2])
    send(E_YR[2], True)
    send(E_YC[2], False)
    self_update(E_XR[0], D_VXR, None)
    self_update(E_XC[0], D_VXC, b_vx)
    self_sums(x_own, b_vx, D_VXR, E_XR[1], E_XC[1])
    send(E_XR[1], True)
    send(E_XC[1], False)

    cross_update(E_XY[3], D_G, b_g)
    partial_lse(a_row, b_g, E_XY[4])
    send(E_XY[4], True)

    self_update(E_YR[2], D_VYR, None)
    self_update(E_YC[2], D_VYC, b_vy)
    moved(1, plan_yy, yr)
    self_update(E_XR[1], D_VXR, None)
    self_update(E_XC[1], D_VXC, None)
    self_sums(x_own, None, D_VXR, None, E_XC[2])
    send(E_XC[2], False)

    cross_update(E_XY[4], D_F, b_f)
    partial_lse(a_col, b_f, E_XY[5])
    dense[D_G] = msg[E_XY[5]]
    used = lax.broadcasted_iota(jnp.int32, (8, LANES), 0) < tiles
    here = jnp.where(used, dense[D_F] - dense[D_NX] - dense[D_NY] - log2(dense[D_VYR]), 0.0)
    msg[E_XY[5], tiles : tiles + 1, :] = jnp.sum(here, 0, keepdims=True)
    send(E_XY[5], False)
    spread(D_G, b_g)
    moved(0, plan_xy, xr)
    self_update(E_XC[2], D_VXC, None)

    receive(E_XY[5])
    parts = got[E_XY[5]]
    lse = combined(E_XY[5])
    msg[E_SUM] = jnp.where(used, log_n - lse - log2(dense[D_VXC]), 0.0)
    send(E_SUM, True)
    weights[...] = jnp.exp2(parts - lse[None])
    others = jnp.sum(parts, 0)[tiles : tiles + 1, :]
    for k in range(tiles):
        rows = jnp.concatenate([weights[:, k, :], jnp.zeros((LANES - GROUP, LANES), jnp.float32)], 0)
        own_w[pl.ds(k * LANES, LANES), :] = rows.T
    mine = own_w[pl.ds(pl.multiple_of(plane_me * shard, 16), shard), :]

    wait_bytes(o_got.at[1, pl.ds(0, GROUP - 1)], bulk_recv.at[5])
    grad = jnp.sum(o_got[1].astype(jnp.float32), 0)
    wait_bytes(o_got.at[0, pl.ds(0, GROUP - 1)], bulk_recv.at[4])
    for n in range(GROUP):
        grad = grad - mine[:, n : n + 1] * o_got[0, n].astype(jnp.float32)
    grad_ref[...] = grad

    receive(E_SUM)
    total = jnp.sum(jnp.sum(got[E_SUM], 0), 0, keepdims=True) + others
    div_ref[...] = jnp.broadcast_to(
        jnp.sum(total, 1, keepdims=True) * (1.0 / (LOG2E * points)), div_ref.shape
    )

    for which, (column, rowwise) in enumerate(((yc, xr), (xc, yr))):
        wait_bytes(column.at[pl.ds(0, 15 * shard)], bulk_send.at[which])
        wait_bytes(rowwise.at[pl.ds(0, 15 * shard)], bulk_send.at[2 + which])
    for index in range(2):
        wait_bytes(o_got.at[index, pl.ds(0, GROUP - 1)], bulk_send.at[4 + index])
    for ex in range(N_EX):
        wait_bytes(got.at[ex, pl.ds(0, GROUP - 1)], ex_send.at[ex])


def shards(x_obs, y_gen):
    shard, width = x_obs.shape
    block = shard * GROUP
    tiles = block // LANES
    f32, bf16 = jnp.float32, jnp.bfloat16
    div, grad = pl.pallas_call(
        kernel,
        out_shape=(jax.ShapeDtypeStruct((8, LANES), f32), jax.ShapeDtypeStruct((shard, width), f32)),
        in_specs=[pl.BlockSpec(memory_space=pltpu.HBM)] * 2,
        out_specs=(pl.BlockSpec(memory_space=pltpu.VMEM), pl.BlockSpec(memory_space=pltpu.VMEM)),
        scratch_shapes=[
            *[pltpu.VMEM((block, width), bf16)] * 4,
            *[pltpu.VMEM((tiles, block, LANES), f32)] * 4,
            *[pltpu.VMEM((block, LANES), f32)] * 6,
            pltpu.VMEM((8, 8, LANES), f32),
            pltpu.VMEM((N_EX, 8, LANES), f32),
            pltpu.VMEM((N_EX, GROUP, 8, LANES), f32),
            pltpu.VMEM((GROUP, 8, LANES), f32),
            pltpu.VMEM((block, LANES), f32),
            pltpu.VMEM((2, block, width), bf16),
            pltpu.VMEM((2, GROUP, shard, width), bf16),
            pltpu.SemaphoreType.DMA((4,)),
            pltpu.SemaphoreType.DMA((6,)),
            pltpu.SemaphoreType.DMA((6,)),
            pltpu.SemaphoreType.DMA((2, 7)),
            pltpu.SemaphoreType.DMA((N_EX,)),
            pltpu.SemaphoreType.DMA((N_EX,)),
        ],
        compiler_params=pltpu.CompilerParams(
            collective_id=0, has_side_effects=True, vmem_limit_bytes=48 * 1024 * 1024
        ),
    )(x_obs, y_gen)
    return div[0, 0], grad


def solution(mesh):
    placed = P(("rows", "cols"), None)
    return jax.shard_map(
        shards, mesh=mesh, in_specs=(placed, placed), out_specs=(P(), placed), check_vma=False
    )
```

time: 81.5 us -> 62.4 us (0.77)
  Pallas kernels: 78.1 us -> 58.8 us
    pallas_call x1, Pallas kernels: 78.1 us -> 58.8 us  [shards(): pl.pallas_call(kernel, out_shape=(jax.ShapeDtypeStruct((8, LANES), f32),...]
where the time goes in v2:
time: 62.4 us; the launch traced here: 62.1 us
  Pallas kernels  58.8 us (94%)
  local copies, waits for them, and re-layouts  2.6 us (4%)
  between operations  0.65 us (1%)
    pallas_call x1, Pallas kernels, shards(): pl.pallas_call(kernel, out_shape=(jax.ShapeDtypeStruct((8, LANES), f32),...  58.8 us
    unnamed x5, local copies, waits for them, and re-layouts  2.09 us

profile of v2, /device:TPU:1, one launch (start us, length us, event | category | flops | bytes accessed | tf_op | source)
XLA Modules:
  0.0 62.1 jit_solution(11275011603523444914)
XLA Ops:
  0.6 0.0 copy-start
  0.6 0.7 %copy-done = bf16[48,256]{1,0:T(8,128)(2,1)S(1)} copy-done((bf16[48,256]{1,0:T(8,128)(2,1)S(1)}, bf16[48,256]{1,0:T(8,128)(2,1)}, u32[]{:S(2)}) %copy-start) | copy-done | bytes 24600
  1.4 0.0 copy-start.1
  1.4 0.7 %copy-done.1 = bf16[48,256]{1,0:T(8,128)(2,1)S(1)} copy-done((bf16[48,256]{1,0:T(8,128)(2,1)S(1)}, bf16[48,256]{1,0:T(8,128)(2,1)}, u32[]{:S(2)}) %copy-start.1) | copy-done | bytes 24600
  2.1 58.8 %shard_map.41 = (f32[8,128]{1,0:T(8,128)S(1)}, f32[48,256]{1,0:T(8,128)S(1)}) custom-call(bf16[48,256]{1,0:T(8,128)(2,1)S(1)} %copy-done, bf16[48,256]{1,0:T(8,128)(2,1)S(1)} %copy-done.1), custom_call_target="tpu_custom_call" | custom-call | tf_op jit(solution)/shard_map/pallas_call | solution.py:396
  60.9 0.5 slice.3
  61.4 0.6 copy.5
Async XLA Ops:
  0.6 0.7 %copy-start = (bf16[48,256]{1,0:T(8,128)(2,1)S(1)}, bf16[48,256]{1,0:T(8,128)(2,1)}, u32[]{:S(2)}) copy-start(bf16[48,256]{1,0:T(8,128)(2,1)} %x_ref.1) | copy-start | bytes 73732
  1.4 0.7 %copy-start.1 = (bf16[48,256]{1,0:T(8,128)(2,1)S(1)}, bf16[48,256]{1,0:T(8,128)(2,1)}, u32[]{:S(2)}) copy-start(bf16[48,256]{1,0:T(8,128)(2,1)} %y_ref.1) | copy-start | bytes 73732

commit v3 on v2

--- a/solution.py
+++ b/solution.py
@@ -16,11 +16,11 @@
 
 E_XY = (0, 1, 2, 3, 4, 5)
 E_YR = (6, 7, 8)
-E_YC = (9, 10, 11)
-E_XR = (12, 13)
-E_XC = (14, 15, 16)
-E_SUM = 17
-N_EX = 18
+E_YC = (9, 10)
+E_XR = (11, 12)
+E_XC = (13, 14, 15)
+E_SUM = 16
+N_EX = 17
 
 
 def log2(value):
@@ -32,7 +32,7 @@
     xr, xc, yr, yc,
     a_col, a_row, y_own, x_own,
     b_f, b_g, b_ny, b_nx, b_vy, b_vx,
-    dense, msg, got, weights, own_w, o_send, o_got,
+    dense, msg, got, sum_msg, sum_got, o_send, o_got,
     local_sem, bulk_send, bulk_recv, line_recv, ex_send, ex_recv,
 ):
     shard = xr.shape[0] // GROUP
@@ -207,7 +207,7 @@
 
         lax.fori_loop(0, tiles // together, step, 0)
 
-    def self_sums(kernel_ref, v_column, v_row, ex_row, ex_col):
+    def tile_sums(tile_ref, v_column, v_row, ex_row, ex_col):
         part, together = 32, 3
 
         def step(first, carry):
@@ -219,13 +219,15 @@
                     rows = pl.ds(pl.multiple_of(n * LANES + g * part, part), part)
                     total = None
                     for k in range(tiles):
-                        tile = kernel_ref[k, rows, :]
+                        tile = tile_ref[k, rows, :]
                         if ex_row is not None:
                             down[k] = down[k] + jnp.sum((tile * v_column[rows, :]).reshape(part // 8, 8, LANES), 0)
-                        term = tile * dense[v_row, k : k + 1, :]
-                        total = term if total is None else total + term
+                        if ex_col is not None:
+                            term = tile * dense[v_row, k : k + 1, :]
+                            total = term if total is None else total + term
                     across.append(total)
-                msg[ex_col, pl.ds(n, 1), :] = jnp.sum(jnp.concatenate(across, 0).T, 0, keepdims=True)
+                if ex_col is not None:
+                    msg[ex_col, pl.ds(n, 1), :] = jnp.sum(jnp.concatenate(across, 0).T, 0, keepdims=True)
             return tuple(down)
 
         first = tuple(jnp.zeros((8, LANES), jnp.float32) for _ in range(tiles if ex_row is not None else 0))
@@ -233,11 +235,36 @@
         for k, value in enumerate(down):
             msg[ex_row, k : k + 1, :] = jnp.sum(value, 0, keepdims=True)
 
-    D_F, D_G, D_NX, D_NY, D_VXR, D_VXC, D_VYR, D_VYC = range(8)
+    def scaled_tile(scores, potential, index, ex):
+        part, together = 64, 3
+
+        def step(first, carry):
+            total = [jnp.zeros((8, LANES), jnp.float32)] * together
+            for n in range(block // part):
+                rows = pl.ds(n * part, part)
+                p = potential[rows, :]
+                for u in range(together):
+                    k = first * together + u
+                    tile = jnp.exp2(scores[k, rows, :] + p + dense[index, pl.ds(k, 1), :])
+                    scores[k, rows, :] = tile
+                    total[u] = total[u] + jnp.sum(tile.reshape(part // 8, 8, LANES), 0)
+            for u in range(together):
+                msg[ex, pl.ds(first * together + u, 1), :] = jnp.sum(total[u], 0, keepdims=True)
+            return carry
+
+        lax.fori_loop(0, tiles // together, step, 0)
+
+    D_F, D_G, D_NX, D_NY, D_VXR, D_VXC, D_VYR, D_VYC, D_U, D_V = range(10)
 
     def cross_update(ex, index, out):
         receive(ex)
         dense[index] = log_n - combined(ex)
+        if out is not None:
+            spread(index, out)
+
+    def scale_update(ex, index, out):
+        receive(ex)
+        dense[index] = points / jnp.sum(got[ex], 0)
         if out is not None:
             spread(index, out)
 
@@ -269,10 +296,10 @@
         o_got[index, plane_me] = o_send[index, pl.ds(pl.multiple_of(plane_me * shard, 16), shard), :]
 
     def plan_yy(k, rows):
-        return y_own[k, rows, :] * (dense[D_VYR, k : k + 1, :] * (1.0 / points)) * b_vy[rows, :]
+        return y_own[k, rows, :] * dense[D_VYR, k : k + 1, :]
 
     def plan_xy(k, rows):
-        return jnp.exp2(a_row[k, rows, :] + dense[D_F, k : k + 1, :] - b_g[rows, :])
+        return a_row[k, rows, :] * dense[D_U, k : k + 1, :]
 
     gather(0, yc, xr)
     gather(1, None, yr)
@@ -291,7 +318,7 @@
     gather_line(1, yr)
     half_norms(yr, None, D_NY)
     products(yc, yr, y_own, b_ny, D_NY)
-    self_sums(y_own, b_vy, D_VYR, E_YR[0], E_YC[0])
+    tile_sums(y_own, b_vy, D_VYR, E_YR[0], E_YC[0])
     send(E_YR[0], True)
     send(E_YC[0], False)
 
@@ -302,79 +329,76 @@
     gather_plane(1, xc)
     half_norms(xc, b_nx, None)
     products(xc, xr, x_own, b_nx, D_NX)
-    self_sums(x_own, b_vx, D_VXR, E_XR[0], E_XC[0])
+    self_update(E_YR[0], D_VYR, None)
+    self_update(E_YC[0], D_VYC, b_vy)
+    tile_sums(y_own, b_vy, D_VYR, E_YR[1], E_YC[1])
+    send(E_YR[1], True)
+    send(E_YC[1], False)
+
+    cross_update(E_XY[1], D_G, b_g)
+    scaled_tile(a_row, b_g, D_F, E_XY[2])
+    send(E_XY[2], True)
+
+    tile_sums(x_own, b_vx, D_VXR, E_XR[0], E_XC[0])
     send(E_XR[0], True)
     send(E_XC[0], False)
-
-    cross_update(E_XY[1], D_G, b_g)
-    partial_lse(a_row, b_g, E_XY[2])
-    send(E_XY[2], True)
-
-    self_update(E_YR[0], D_VYR, None)
-    self_update(E_YC[0], D_VYC, b_vy)
-    self_sums(y_own, b_vy, D_VYR, E_YR[1], E_YC[1])
-    send(E_YR[1], True)
-    send(E_YC[1], False)
-
-    cross_update(E_XY[2], D_F, b_f)
-    partial_lse(a_col, b_f, E_XY[3])
-    send(E_XY[3], False)
-
     self_update(E_YR[1], D_VYR, None)
     self_update(E_YC[1], D_VYC, b_vy)
-    self_sums(y_own, b_vy, D_VYR, E_YR[2], E_YC[2])
+    tile_sums(y_own, b_vy, None, E_YR[2], None)
     send(E_YR[2], True)
-    send(E_YC[2], False)
+
+    scale_update(E_XY[2], D_U, None)
+    tile_sums(a_row, None, D_U, None, E_XY[3])
+    send(E_XY[3], False)
+
     self_update(E_XR[0], D_VXR, None)
     self_update(E_XC[0], D_VXC, b_vx)
-    self_sums(x_own, b_vx, D_VXR, E_XR[1], E_XC[1])
+    tile_sums(x_own, b_vx, D_VXR, E_XR[1], E_XC[1])
     send(E_XR[1], True)
     send(E_XC[1], False)
 
-    cross_update(E_XY[3], D_G, b_g)
-    partial_lse(a_row, b_g, E_XY[4])
+    scale_update(E_XY[3], D_V, b_g)
+    tile_sums(a_row, b_g, None, E_XY[4], None)
     send(E_XY[4], True)
 
     self_update(E_YR[2], D_VYR, None)
-    self_update(E_YC[2], D_VYC, b_vy)
     moved(1, plan_yy, yr)
     self_update(E_XR[1], D_VXR, None)
     self_update(E_XC[1], D_VXC, None)
-    self_sums(x_own, None, D_VXR, None, E_XC[2])
+    tile_sums(x_own, None, D_VXR, None, E_XC[2])
     send(E_XC[2], False)
 
-    cross_update(E_XY[4], D_F, b_f)
-    partial_lse(a_col, b_f, E_XY[5])
-    dense[D_G] = msg[E_XY[5]]
+    scale_update(E_XY[4], D_U, None)
+    tile_sums(a_row, None, D_U, None, E_XY[5])
     used = lax.broadcasted_iota(jnp.int32, (8, LANES), 0) < tiles
-    here = jnp.where(used, dense[D_F] - dense[D_NX] - dense[D_NY] - log2(dense[D_VYR]), 0.0)
+    here = jnp.where(used, dense[D_F] + log2(dense[D_U] / dense[D_VYR]) - dense[D_NX] - dense[D_NY], 0.0)
     msg[E_XY[5], tiles : tiles + 1, :] = jnp.sum(here, 0, keepdims=True)
     send(E_XY[5], False)
-    spread(D_G, b_g)
     moved(0, plan_xy, xr)
     self_update(E_XC[2], D_VXC, None)
 
-    receive(E_XY[5])
-    parts = got[E_XY[5]]
-    lse = combined(E_XY[5])
-    msg[E_SUM] = jnp.where(used, log_n - lse - log2(dense[D_VXC]), 0.0)
-    send(E_SUM, True)
-    weights[...] = jnp.exp2(parts - lse[None])
-    others = jnp.sum(parts, 0)[tiles : tiles + 1, :]
-    for k in range(tiles):
-        rows = jnp.concatenate([weights[:, k, :], jnp.zeros((LANES - GROUP, LANES), jnp.float32)], 0)
-        own_w[pl.ds(k * LANES, LANES), :] = rows.T
-    mine = own_w[pl.ds(pl.multiple_of(plane_me * shard, 16), shard), :]
+    scale_update(E_XY[5], D_V, None)
+    here = jnp.where(used, dense[D_G] + log2(dense[D_V] / dense[D_VXC]), 0.0)
+    sum_msg[...] = jnp.sum(here, 0, keepdims=True)
+    for peer in line_at:
+        send_to(sum_msg, sum_got.at[line_me], ex_send.at[E_SUM], ex_recv.at[E_SUM], peer)
+    sum_got[line_me] = sum_msg[...]
+    others = jnp.sum(got[E_XY[5], :, tiles : tiles + 1, :], 0)
+    spread(D_V, b_f)
+    spread(D_VYR, b_vy)
+    mine_xy = b_f[pl.ds(pl.multiple_of(plane_me * shard, 16), shard), :] * (1.0 / points)
+    mine_yy = b_vy[pl.ds(pl.multiple_of(line_me * shard, 16), shard), :] * (1.0 / points)
 
     wait_bytes(o_got.at[1, pl.ds(0, GROUP - 1)], bulk_recv.at[5])
-    grad = jnp.sum(o_got[1].astype(jnp.float32), 0)
+    moved_yy = jnp.sum(o_got[1].astype(jnp.float32), 0)
     wait_bytes(o_got.at[0, pl.ds(0, GROUP - 1)], bulk_recv.at[4])
-    for n in range(GROUP):
-        grad = grad - mine[:, n : n + 1] * o_got[0, n].astype(jnp.float32)
-    grad_ref[...] = grad
-
-    receive(E_SUM)
-    total = jnp.sum(jnp.sum(got[E_SUM], 0), 0, keepdims=True) + others
+    moved_xy = jnp.sum(o_got[0].astype(jnp.float32), 0)
+    grad_ref[...] = (
+        jnp.concatenate([mine_yy, mine_yy], 1) * moved_yy - jnp.concatenate([mine_xy, mine_xy], 1) * moved_xy
+    )
+
+    wait_bytes(sum_got.at[pl.ds(0, GROUP - 1)], ex_recv.at[E_SUM])
+    total = jnp.sum(sum_got[...], 0) + others
     div_ref[...] = jnp.broadcast_to(
         jnp.sum(total, 1, keepdims=True) * (1.0 / (LOG2E * points)), div_ref.shape
     )
@@ -384,7 +408,8 @@
         wait_bytes(rowwise.at[pl.ds(0, 15 * shard)], bulk_send.at[2 + which])
     for index in range(2):
         wait_bytes(o_got.at[index, pl.ds(0, GROUP - 1)], bulk_send.at[4 + index])
-    for ex in range(N_EX):
+    wait_bytes(sum_got.at[pl.ds(0, GROUP - 1)], ex_send.at[E_SUM])
+    for ex in range(E_SUM):
         wait_bytes(got.at[ex, pl.ds(0, GROUP - 1)], ex_send.at[ex])
 
 
@@ -402,11 +427,11 @@
             *[pltpu.VMEM((block, width), bf16)] * 4,
             *[pltpu.VMEM((tiles, block, LANES), f32)] * 4,
             *[pltpu.VMEM((block, LANES), f32)] * 6,
-            pltpu.VMEM((8, 8, LANES), f32),
+            pltpu.VMEM((10, 8, LANES), f32),
             pltpu.VMEM((N_EX, 8, LANES), f32),
             pltpu.VMEM((N_EX, GROUP, 8, LANES), f32),
-            pltpu.VMEM((GROUP, 8, LANES), f32),
-            pltpu.VMEM((block, LANES), f32),
+            pltpu.VMEM((1, LANES), f32),
+            pltpu.VMEM((GROUP, 1, LANES), f32),
             pltpu.VMEM((2, block, width), bf16),
             pltpu.VMEM((2, GROUP, shard, width), bf16),
             pltpu.SemaphoreType.DMA((4,)),

time: 62.4 us -> 59.9 us (0.960)
  Pallas kernels: 58.8 us -> 56.4 us
    pallas_call x1, Pallas kernels: 58.8 us -> 56.4 us  [shards(): pl.pallas_call(kernel, out_shape=(jax.ShapeDtypeStruct((8, LANES), f32),...]
where the time goes in v3:
time: 59.9 us; the launch traced here: 59.7 us
  Pallas kernels  56.4 us (94%)
  local copies, waits for them, and re-layouts  2.6 us (4%)
  between operations  0.65 us (1%)
    pallas_call x1, Pallas kernels, shards(): pl.pallas_call(kernel, out_shape=(jax.ShapeDtypeStruct((8, LANES), f32),...  56.4 us
    unnamed x5, local copies, waits for them, and re-layouts  2.09 us

profile of v3, /device:TPU:1, one launch (start us, length us, event | category | flops | bytes accessed | tf_op | source)
XLA Modules:
  0.0 59.7 jit_solution(17550316007161722408)
XLA Ops:
  0.6 0.0 copy-start
  0.6 0.7 %copy-done = bf16[48,256]{1,0:T(8,128)(2,1)S(1)} copy-done((bf16[48,256]{1,0:T(8,128)(2,1)S(1)}, bf16[48,256]{1,0:T(8,128)(2,1)}, u32[]{:S(2)}) %copy-start) | copy-done | bytes 24600
  1.4 0.0 copy-start.1
  1.4 0.7 %copy-done.1 = bf16[48,256]{1,0:T(8,128)(2,1)S(1)} copy-done((bf16[48,256]{1,0:T(8,128)(2,1)S(1)}, bf16[48,256]{1,0:T(8,128)(2,1)}, u32[]{:S(2)}) %copy-start.1) | copy-done | bytes 24600
  2.1 56.4 %shard_map.41 = (f32[8,128]{1,0:T(8,128)S(1)}, f32[48,256]{1,0:T(8,128)S(1)}) custom-call(bf16[48,256]{1,0:T(8,128)(2,1)S(1)} %copy-done, bf16[48,256]{1,0:T(8,128)(2,1)S(1)} %copy-done.1), custom_call_target="tpu_custom_call" | custom-call | tf_op jit(solution)/shard_map/pallas_call | solution.py:421
  58.5 0.5 slice.3
  59.0 0.6 %copy.5 = f32[48,256]{1,0:T(8,128)} copy(f32[48,256]{1,0:T(8,128)S(1)} %get-tuple-element.9) | data formatting | bytes 98304
Async XLA Ops:
  0.6 0.7 %copy-start = (bf16[48,256]{1,0:T(8,128)(2,1)S(1)}, bf16[48,256]{1,0:T(8,128)(2,1)}, u32[]{:S(2)}) copy-start(bf16[48,256]{1,0:T(8,128)(2,1)} %x_ref.1) | copy-start | bytes 73732
  1.4 0.7 %copy-start.1 = (bf16[48,256]{1,0:T(8,128)(2,1)S(1)}, bf16[48,256]{1,0:T(8,128)(2,1)}, u32[]{:S(2)}) copy-start(bf16[48,256]{1,0:T(8,128)(2,1)} %y_ref.1) | copy-start | bytes 73732

commit v4 on v3

--- a/solution.py
+++ b/solution.py
@@ -166,9 +166,9 @@
             for k in range(tiles):
                 dense[index, k : k + 1, :] = value[0:1, k * LANES : (k + 1) * LANES]
 
-    def products(left, right, out, norm_left=None, norm_right=None):
+    def products(left, right, out, norm_left=None, norm_right=None, pairs=range(0, tiles, 2)):
         wide = 2 * LANES
-        for k in range(0, tiles, 2):
+        for k in pairs:
             both = LOG2E * lax.dot_general(
                 left[...],
                 right[k * LANES : k * LANES + wide, :],
@@ -180,6 +180,25 @@
                 if norm_left is not None:
                     part = jnp.exp2(part + norm_left[...] + dense[norm_right, k + h : k + h + 1, :])
                 out[k + h] = part
+
+    def reduce_tiles(scores, potential, ex, which):
+        part = 64
+        state = [None] * len(which)
+        for n in range(block // part):
+            rows = pl.ds(n * part, part)
+            p = potential[rows, :]
+            for u, k in enumerate(which):
+                s = (scores[k, rows, :] + p).reshape(part // 8, 8, LANES)
+                peak = jnp.max(s, 0)
+                total = jnp.sum(jnp.exp2(s - peak[None]), 0)
+                if n:
+                    both = jnp.maximum(state[u][0], peak)
+                    total = state[u][1] * jnp.exp2(state[u][0] - both) + total * jnp.exp2(peak - both)
+                    peak = both
+                state[u] = (peak, total)
+        for (peak, total), k in zip(state, which):
+            top = jnp.max(peak, 0, keepdims=True)
+            msg[ex, k : k + 1, :] = top + log2(jnp.sum(total * jnp.exp2(peak - top), 0, keepdims=True))
 
     def partial_lse(scores, potential, ex):
         part, together = 64, 3
@@ -307,8 +326,9 @@
     gather_plane(0, yc)
     half_norms(yc, b_ny, None)
     gather_line(0, xr)
-    products(yc, xr, a_row)
-    partial_lse(a_row, b_ny, E_XY[0])
+    for first in range(0, tiles, 2):
+        products(yc, xr, a_row, pairs=(first,))
+        reduce_tiles(a_row, b_ny, E_XY[0], (first, first + 1))
     send(E_XY[0], True)
 
     gather(1, xc, None)

time: 59.9 us -> 59.7 us (level)
  no operation moved by 1% of the time
where the time goes in v4:
time: 59.7 us; the launch traced here: 59.5 us
  Pallas kernels  56.2 us (94%)
  local copies, waits for them, and re-layouts  2.6 us (4%)
  between operations  0.65 us (1%)
    pallas_call x1, Pallas kernels, shards(): pl.pallas_call(kernel, out_shape=(jax.ShapeDtypeStruct((8, LANES), f32),...  56.2 us
    unnamed x5, local copies, waits for them, and re-layouts  2.09 us

profile of v4, /device:TPU:1, one launch (start us, length us, event | category | flops | bytes accessed | tf_op | source)
XLA Modules:
  0.0 59.5 jit_solution(8567208107026348154)
XLA Ops:
  0.6 0.0 copy-start
  0.6 0.7 %copy-done = bf16[48,256]{1,0:T(8,128)(2,1)S(1)} copy-done((bf16[48,256]{1,0:T(8,128)(2,1)S(1)}, bf16[48,256]{1,0:T(8,128)(2,1)}, u32[]{:S(2)}) %copy-start) | copy-done | bytes 24600
  1.4 0.0 copy-start.1
  1.4 0.7 %copy-done.1 = bf16[48,256]{1,0:T(8,128)(2,1)S(1)} copy-done((bf16[48,256]{1,0:T(8,128)(2,1)S(1)}, bf16[48,256]{1,0:T(8,128)(2,1)}, u32[]{:S(2)}) %copy-start.1) | copy-done | bytes 24600
  2.1 56.2 %shard_map.41 = (f32[8,128]{1,0:T(8,128)S(1)}, f32[48,256]{1,0:T(8,128)S(1)}) custom-call(bf16[48,256]{1,0:T(8,128)(2,1)S(1)} %copy-done, bf16[48,256]{1,0:T(8,128)(2,1)S(1)} %copy-done.1), custom_call_target="tpu_custom_call" | custom-call | tf_op jit(solution)/shard_map/pallas_call | solution.py:441
  58.3 0.5 slice.3
  58.8 0.6 %copy.5 = f32[48,256]{1,0:T(8,128)} copy(f32[48,256]{1,0:T(8,128)S(1)} %get-tuple-element.9) | data formatting | bytes 98304
Async XLA Ops:
  0.6 0.7 %copy-start = (bf16[48,256]{1,0:T(8,128)(2,1)S(1)}, bf16[48,256]{1,0:T(8,128)(2,1)}, u32[]{:S(2)}) copy-start(bf16[48,256]{1,0:T(8,128)(2,1)} %x_ref.1) | copy-start | bytes 73732
  1.4 0.7 %copy-start.1 = (bf16[48,256]{1,0:T(8,128)(2,1)S(1)}, bf16[48,256]{1,0:T(8,128)(2,1)}, u32[]{:S(2)}) copy-start(bf16[48,256]{1,0:T(8,128)(2,1)} %y_ref.1) | copy-start | bytes 73732
